TPU v7x, 256 devices: a whole 4x4x8 slice. The times are simulated.
256 devices in a mesh: section: 8 (over x, core), expert: 32 (over y, z).
Axes of the slice: x: 4, y: 4, z: 8, core: 2. Of those that a mesh axis runs over, the one named last changes fastest.
Arguments:
- hidden: bfloat16 [8, 2048, 7168], P('section', 'expert'), may hold values from -6 to 6
- norm_gain: float32 [8, 7168], P('section'), may hold values from 0.5 to 1.5
- gate_weight: bfloat16 [8, 7168, 8192], P('section', None, 'expert'), may hold values from -0.0625 to 0.0625
- up_weight: bfloat16 [8, 7168, 8192], P('section', None, 'expert'), may hold values from -0.0625 to 0.0625
- down_weight: bfloat16 [8, 8192, 7168], P('section', 'expert'), may hold values from -0.1875 to 0.1875
- routes: int32 [8, 2048, 2], P('section', 'expert'), may hold values from 0 to 7, all different within a row; in each aligned block of 64 rows (0 to 63, 64 to 127, ..., all dimensions but the last counted through in order) at most 32 rows name the same one
- logits: float32 [8, 2048, 2], P('section', 'expert'), may hold values from -8 to 8
Outputs:
- mixed: bfloat16 [8, 2048, 7168], P('section', 'expert')
Inputs may be any that keep to these rules, and one draw needn't show every extreme that they name: `routes`: each token names 2 different experts. Among the 64 tokens of one device, no expert is named more than 32 times; in every draw the tokens of some device name some expert exactly 32 times.
All inputs are finite; a program needn't handle non-finite values.
Results may differ from a plain program's by a relative error of at most 0.0061.
Values may be sent and summed in bfloat16 or wider, within the bound.
No kernel may reach another device: no remote copies, remote signals or barrier semaphores. Data moves between devices by JAX's collectives and lax.ppermute only.
A program may use at most 192 MiB of HBM per device.

v0:
```python
import jax
import jax.numpy as jnp
from jax import lax
from jax.sharding import PartitionSpec as P

SLICES = 4


ROUTE_SCALE = 2.5
EPSILON = 1e-06


def passed_along(x, axis, by):
    size = lax.axis_size(axis)
    return lax.ppermute(x, axis, [(i, (i + by) % size) for i in range(size)])


def rms_normed(values, gain_row):
    widened = values.astype(jnp.float32)
    scaled = lax.rsqrt(jnp.mean(widened * widened, axis=-1, keepdims=True) + EPSILON)
    return (widened * scaled * gain_row).astype(jnp.bfloat16)


def route_weights(scores):
    gate_values = jax.nn.sigmoid(scores)
    return ROUTE_SCALE * gate_values / jnp.sum(gate_values, axis=-1, keepdims=True)


def per_device(hidden, norm_gain, gate_weight, up_weight, down_weight, routes, logits):
    arrived = passed_along(hidden[0], "section", 1)
    normed = rms_normed(arrived, norm_gain[0])
    token_count = routes.shape[1]
    top_count = routes.shape[2]
    model_width = hidden.shape[2]
    groups = lax.axis_size("expert") // SLICES
    most_rows = min(token_count, 2 * token_count * top_count // groups)
    slot_count = groups * most_rows
    w_gate = gate_weight[0]
    w_up = up_weight[0]
    w_down = down_weight[0]
    flat_routes = routes[0].reshape(token_count * top_count)
    expert_hits = (flat_routes[:, None] == jnp.arange(groups, dtype=jnp.int32)[None, :]).astype(
        jnp.int32
    )
    ranked = jnp.cumsum(expert_hits, axis=0) - expert_hits
    slot_index = jnp.sum(ranked * expert_hits, axis=1)
    destination = flat_routes * most_rows + slot_index
    picked = (destination[:, None] == jnp.arange(slot_count, dtype=jnp.int32)[None, :]).astype(
        jnp.float32
    )
    picked = picked.reshape(token_count, top_count, slot_count)
    select_rows = jnp.sum(picked, axis=1).astype(jnp.bfloat16)
    combine_rows = jnp.sum(picked * route_weights(logits[0])[:, :, None], axis=1)
    slot_rows = jnp.einsum(
        "tq,td->qd", select_rows, normed, preferred_element_type=jnp.float32
    ).astype(jnp.bfloat16)
    outgoing = jnp.broadcast_to(
        slot_rows.reshape(groups, 1, most_rows, model_width),
        (groups, SLICES, most_rows, model_width),
    )
    outgoing = outgoing.reshape(groups * SLICES, most_rows, model_width)
    pair_rows = lax.all_to_all(outgoing, "expert", split_axis=0, concat_axis=0, tiled=True)
    gate_proj = jnp.einsum("smd,df->smf", pair_rows, w_gate, preferred_element_type=jnp.float32)
    up_proj = jnp.einsum("smd,df->smf", pair_rows, w_up, preferred_element_type=jnp.float32)
    activated = (jax.nn.silu(gate_proj) * up_proj).astype(jnp.bfloat16)
    partials = jnp.einsum("smf,fd->smd", activated, w_down, preferred_element_type=jnp.float32)
    returned = lax.all_to_all(partials, "expert", split_axis=0, concat_axis=0, tiled=True)
    slot_weights = combine_rows.reshape(token_count, groups, most_rows)
    expert_output = jnp.sum(
        returned.reshape(groups, SLICES, most_rows, model_width), axis=1
    ).astype(jnp.bfloat16)
    expert_output = lax.optimization_barrier(expert_output).astype(jnp.float32)
    routed_sum = jnp.einsum(
        "tem,emd->td", slot_weights, expert_output, precision=lax.Precision.HIGHEST
    )
    mixed = (arrived.astype(jnp.float32) + routed_sum).astype(jnp.bfloat16)
    return mixed[None]


def solution(mesh):
    in_specs = (
        P("section", "expert", None),
        P("section", None),
        P("section", None, "expert"),
        P("section", None, "expert"),
        P("section", "expert", None),
        P("section", "expert", None),
        P("section", "expert", None),
    )
    out_specs = P("section", "expert", None)
    return jax.shard_map(
        per_device, mesh=mesh, in_specs=in_specs, out_specs=out_specs, check_vma=False
    )
```

profile of v0, /device:TPU:188, one launch (start us, length us, event | category | flops | bytes accessed | tf_op | source)
XLA Modules:
  0.0 1132.3 jit_solution(15192759346185260626)
XLA Ops:
  0.0 0.0 collective-permute-start
  0.0 0.8 copy.19
  0.8 0.1 eq.29
  0.9 0.1 fusion.29
  1.0 0.2 reduce_window_sum.11
  1.2 0.2 select_reduce_fusion.1
  1.4 0.1 reduce_sum.57
  1.5 0.1 copy.20
  1.6 0.7 fusion.32
  2.3 0.7 bitcast_add_fusion
  3.0 0.1 convert_reduce_fusion
  3.1 9.9 collective-permute-done
  13.0 0.3 fusion.9
  13.3 1.9 convolution_convert_fusion
  15.3 1.9 broadcast_in_dim.7
  17.2 0.0 copy-start.1
  17.2 324.7 %all_to_all.10 = bf16[32,32,7168]{2,1,0:T(8,128)(2,1)S(1)} all-to-all(bf16[32,32,7168]{2,1,0:T(8,128)(2,1)S(1)} %bitcast.44), channel_id=1, replica_groups=mesh['section'=8,'expert'=32] {'expert'}, dimensions={0} | all-to-all | bytes 29360128 | tf_op jit(solution)/shard_map/all_to_all | solution.py:62
  341.9 0.0 copy-start
  341.9 5.2 copy-done
  347.1 0.0 copy-done.1
  347.1 3.9 fusion.7
  351.1 25.8 %fusion.3 = f32[32,32,7168]{2,1,0:T(8,128)} fusion(bf16[1,256,7168]{2,1,0:T(8,128)(2,1)} %param.11, bf16[32,32,7168]{2,1,0:T(8,128)(2,1)} %copy-done, bf16[1,7168,256]{2,1,0:T(8,128)(2,1)} %param.10, f32[32,32,256]{2,1,0:T(8,128)S(1)} %fusion.7), kind=kOutput, calls=%fused_computation.6 | convolution fusion | flops 7517765632 | bytes 52428800 | tf_op jit(solution)/shard_map/smf,fd->smd/dot_general | solution.py:66
  376.9 10.2 all-to-all-start.1
  387.1 0.1 copy.21
  387.2 729.9 %all-to-all-done.1 = f32[32,32,7168]{2,1,0:T(8,128)} async-done(((f32[32,32,7168]{2,1,0:T(8,128)}), f32[32,32,7168]{2,1,0:T(8,128)}, u32[]{:S(2)}, u32[]{:S(2)}) %all-to-all-start.1) | async-done | bytes 29360160 | tf_op jit(solution)/shard_map/all_to_all | solution.py:67
  1117.1 12.2 %bitcast_reduce_fusion = bf16[8,32,7168]{2,1,0:T(8,128)(2,1)S(1)} fusion(f32[32,32,7168]{2,1,0:T(8,128)} %all-to-all-done.1), kind=kLoop, calls=%fused_computation | loop fusion | flops 5505024 | bytes 33030144 | tf_op jit(solution)/shard_map/reduce_sum | solution.py:69
  1129.3 3.0 fusion.2
  (2 shorter events, 0.0 us)
Async XLA Ops:
  0.0 13.0 %collective-permute-start = (bf16[64,7168]{1,0:T(8,128)(2,1)}, bf16[64,7168]{1,0:T(8,128)(2,1)S(1)}, u32[]{:S(2)}, u32[]{:S(2)}) collective-permute-start(bf16[64,7168]{1,0:T(8,128)(2,1)} %bitcast.48), channel_id=1, source_target_pairs={{0,32},{32,64},{64,96},{96,128},{128,160},{160,192},{192,224},{224... | collective-permute-start | bytes 2752520 | tf_op jit(solution)/shard_map/ppermute | solution.py:15
  17.2 329.9 %copy-start.1 = (bf16[1,7168,256]{2,1,0:T(8,128)(2,1)S(1)}, bf16[1,7168,256]{2,1,0:T(8,128)(2,1)}, u32[]{:S(2)}) copy-start(bf16[1,7168,256]{2,1,0:T(8,128)(2,1)} %param.9) | copy-start | bytes 11010052
  341.9 5.2 copy-start
  376.9 740.2 %all-to-all-start.1 = ((f32[32,32,7168]{2,1,0:T(8,128)}), f32[32,32,7168]{2,1,0:T(8,128)}, u32[]{:S(2)}, u32[]{:S(2)}) async-start(f32[32,32,7168]{2,1,0:T(8,128)} %fusion.3), calls=%async_computation.1 | async-start | bytes 58720256 | tf_op jit(solution)/shard_map/all_to_all | solution.py:67
where the time goes:
time: 1130 us
  waiting for transfers between devices  740 us (65%)
  blocking collectives  325 us (29%)
  matrix products  34.7 us (3%)
  other arithmetic  14.4 us (1%)
    all_to_all x1, waiting for transfers between devices, per_device(): lax.all_to_all(partials, 'expert', split_axis=0, concat_axis=0, tiled=True)  730 us
    all_to_all x1, blocking collectives, per_device(): lax.all_to_all(outgoing, 'expert', split_axis=0, concat_axis=0, tiled=True)  325 us
    dot_general x1, matrix products, per_device(): jnp.einsum('smf,fd->smd', activated, w_down, preferred_element_type=jnp.f...  25.8 us
  transfers between devices with their start and end apart: 2, of which 2 were waited for; matrix products, arithmetic and copies ran while one was open for 0% of the time, Pallas kernels for 0%

commit v1 on v0

v1 whole, which is shorter than its diff:
```python
import jax
import jax.numpy as jnp
from jax import lax
from jax.sharding import PartitionSpec as P

ROUTE_SCALE = 2.5
EPSILON = 1e-06
NY = 4
NZ = 8


def moved(x, dy, dz):
    pairs = []
    for y in range(NY):
        for z in range(NZ):
            pairs.append((y * NZ + z, ((y + dy) % NY) * NZ + (z + dz) % NZ))
    return lax.ppermute(x, "expert", pairs)


def next_section(x):
    size = lax.axis_size("section")
    return lax.ppermute(x, "section", [(i, (i + 1) % size) for i in range(size)])


def rms_normed(values, gain_row):
    widened = values.astype(jnp.float32)
    scaled = lax.rsqrt(jnp.mean(widened * widened, axis=-1, keepdims=True) + EPSILON)
    return (widened * scaled * gain_row).astype(jnp.bfloat16)


def route_weights(scores):
    gate_values = jax.nn.sigmoid(scores)
    return ROUTE_SCALE * gate_values / jnp.sum(gate_values, axis=-1, keepdims=True)


def dot(a, b):
    return jnp.dot(a, b, preferred_element_type=jnp.float32)


def across_y(x):
    return moved(x, 2, 0)


def per_device(hidden, norm_gain, gate_weight, up_weight, down_weight, routes, logits):
    bf16 = jnp.bfloat16
    me = lax.axis_index("expert")
    y, z = me // NZ, me % NZ
    tokens, width = hidden.shape[1], hidden.shape[2]
    hid = gate_weight.shape[2]
    part = width // NY
    half = part // 2
    experts = lax.axis_size("expert") // 4

    def w_in(weight):
        def rows_for(d):
            return lax.dynamic_slice(weight, (((y + d) % NY) * part, 0), (part, hid))

        return [
            rows_for(0),
            moved(rows_for(3), -1, 0),
            across_y(rows_for(2)),
            moved(rows_for(1), 1, 0),
        ]

    def w_out(weight):
        def cols_for(d):
            return lax.dynamic_slice(weight, (0, ((y + d) % NY) * part), (hid, part))

        return [
            cols_for(0),
            moved(cols_for(3), -1, 0),
            across_y(cols_for(2)),
            moved(cols_for(1), 1, 0),
        ]

    gates = w_in(gate_weight[0])
    ups = w_in(up_weight[0])
    w_gu = [jnp.concatenate([g, u], axis=1) for g, u in zip(gates, ups)]
    w_down = jnp.concatenate(w_out(down_weight[0]), axis=0)

    chosen = (routes[0][:, :, None] == jnp.arange(experts, dtype=jnp.int32)).astype(jnp.float32)
    table = jnp.sum(chosen * route_weights(logits[0])[:, :, None], axis=1)
    table = lax.all_gather(table, "expert", axis=0, tiled=True)
    mine = (jnp.arange(experts) == me // 4).astype(jnp.float32)
    table = jnp.sum(table * mine, axis=1).reshape(NY, NZ, tokens).transpose(1, 0, 2)
    table = jnp.roll(table, -z, axis=0).reshape(NZ, NY * tokens)

    arrived = next_section(hidden[0])
    normed = rms_normed(arrived, norm_gain[0])

    def quarter(d):
        return lax.dynamic_slice(normed, (0, ((y + d) % NY) * part), (tokens, part))

    block = jnp.stack(
        [quarter(0), moved(quarter(3), -1, 0), across_y(quarter(2)), moved(quarter(1), 1, 0)]
    )
    block = jnp.roll(block, y, axis=0).reshape(NY * tokens, part)
    x = {0: block}
    for k in (1, 2, 3):
        x[k] = moved(x[k - 1], 0, -1)
        x[-k] = moved(x[1 - k], 0, 1)
    x[4] = jnp.concatenate(
        [moved(x[3][:, :half], 0, -1), moved(x[-3][:, half:], 0, 1)], axis=1
    )

    def activated(keys):
        rows = [x[k] for k in keys]
        rows = rows[0] if len(rows) == 1 else jnp.concatenate(rows, axis=0)
        weight = jnp.concatenate([table[k % NZ] for k in keys])[:, None]
        far = dot(rows, w_gu[2]).astype(bf16)
        far_up = moved(far[:, :hid], 1, 0)
        far_down = moved(far[:, hid:], -1, 0)
        right = dot(rows, w_gu[1])
        right = right + jnp.pad(far_up.astype(jnp.float32), ((0, 0), (0, hid)))
        left = dot(rows, w_gu[3])
        left = left + jnp.pad(far_down.astype(jnp.float32), ((0, 0), (hid, 0)))
        right = moved(right.astype(bf16), 1, 0).astype(jnp.float32)
        left = moved(left.astype(bf16), -1, 0).astype(jnp.float32)
        total = dot(rows, w_gu[0]) + right + left
        gate, up = total[:, :hid], total[:, hid:]
        act = (jax.nn.silu(gate) * up * weight).astype(bf16)
        acts = jnp.concatenate(
            [act, moved(act, -1, 0), across_y(act), moved(act, 1, 0)], axis=1
        )
        size = NY * tokens
        return {k: acts[i * size : (i + 1) * size] for i, k in enumerate(keys)}

    acts = {}
    for keys in ((4,), (3, -3), (2, -2), (1, -1), (0,)):
        acts.update(activated(keys))

    wide = [w_down[:, :half], w_down[:, half:]]

    def partial(k, c):
        return dot(acts[k], wide[c])

    def homeward(c, sign, steps):
        sent = None
        for k in range(steps, 0, -1):
            term = partial(4 if k == 4 else sign * k, c)
            if sent is not None:
                term = term + sent.astype(jnp.float32)
            sent = moved(term.astype(bf16), 0, sign)
        return sent.astype(jnp.float32)

    sums = []
    for c in (0, 1):
        plus = homeward(c, 1, 4 if c == 0 else 3)
        minus = homeward(c, -1, 3 if c == 0 else 4)
        sums.append((partial(0, c) + plus + minus).astype(bf16))
    sums = jnp.concatenate(sums, axis=1).reshape(NY, tokens, part)

    def rows_for(d):
        return lax.dynamic_index_in_dim(sums, (y + d) % NY, 0, keepdims=False)

    home = jnp.stack(
        [rows_for(0), moved(rows_for(3), -1, 0), across_y(rows_for(2)), moved(rows_for(1), 1, 0)]
    )
    home = jnp.roll(home, y, axis=0).transpose(1, 0, 2).reshape(tokens, width)
    mixed = (arrived.astype(jnp.float32) + home.astype(jnp.float32)).astype(bf16)
    return mixed[None]


def solution(mesh):
    in_specs = (
        P("section", "expert", None),
        P("section", None),
        P("section", None, "expert"),
        P("section", None, "expert"),
        P("section", "expert", None),
        P("section", "expert", None),
        P("section", "expert", None),
    )
    out_specs = P("section", "expert", None)
    return jax.shard_map(
        per_device, mesh=mesh, in_specs=in_specs, out_specs=out_specs, check_vma=False
    )
```

time: 1130 us -> 456 us (0.40)
  the two profiles are of different devices: /device:TPU:188 before, /device:TPU:4 now
where the time goes in v1:
time: 456 us; the launch traced here: 449 us
  waiting for transfers between devices  197 us (43%)
  starting transfers between devices  103 us (23%)
  blocking collectives  94.5 us (21%)
  matrix products  34.3 us (8%)
  local copies, waits for them, and re-layouts  13.7 us (3%)
  other arithmetic  5.48 us (1%)
    ppermute x72, waiting for transfers between devices, moved(): return lax.ppermute(x, 'expert', pairs)  197 us
    ppermute x72, starting transfers between devices, moved(): return lax.ppermute(x, 'expert', pairs)  103 us
    all_gather x1, blocking collectives, per_device(): table = lax.all_gather(table, 'expert', axis=0, tiled=True)  94.5 us
    dot_general x36, matrix products, dot(): return jnp.dot(a, b, preferred_element_type=jnp.float32)  34.3 us
  transfers between devices with their start and end apart: 73, of which 34 were waited for; matrix products, arithmetic and copies ran while one was open for 11% of the time, Pallas kernels for 0%

profile of v1, /device:TPU:4, one launch (start us, length us, event | category | flops | bytes accessed | tf_op | source)
XLA Modules:
  0.0 448.6 jit_solution(13929641878150637568)
XLA Ops:
  0.0 4.1 dynamic-slice_bitcast_fusion.11
  12.4 94.5 %all-gather = f32[32,64,8]{1,2,0:T(8,128)S(1)} all-gather(f32[1,64,8]{1,2,0:T(8,128)S(1)} %bitcast.106), channel_id=1, replica_groups=mesh['section'=8,'expert'=32] {'expert'}, dimensions={0}, use_global_device_ids=true | all-gather | bytes 67584 | tf_op jit(solution)/shard_map/all_gather | solution.py:83
  122.1 13.2 %collective-permute-done.11 = bf16[1792,256]{1,0:T(8,128)(2,1)S(1)} collective-permute-done((bf16[1792,256]{1,0:T(8,128)(2,1)S(1)}, bf16[1792,256]{1,0:T(8,128)(2,1)S(1)}, u32[]{:S(2)}, u32[]{:S(2)}) %collective-permute-start.11) | collective-permute-done | bytes 917536 | tf_op jit(solution)/shard_map/ppermute | solution.py:17
  139.5 39.3 %collective-permute-done.19 = bf16[256,1792]{1,0:T(8,128)(2,1)S(1)} collective-permute-done((bf16[256,1792]{1,0:T(8,128)(2,1)S(1)}, bf16[256,1792]{1,0:T(8,128)(2,1)S(1)}, u32[]{:S(2)}, u32[]{:S(2)}) %collective-permute-start.19) | collective-permute-done | bytes 917536 | tf_op jit(solution)/shard_map/ppermute | solution.py:17
  179.3 11.7 %collective-permute-done.7 = bf16[1792,256]{1,0:T(8,128)(2,1)S(1)} collective-permute-done((bf16[1792,256]{1,0:T(8,128)(2,1)S(1)}, bf16[1792,256]{1,0:T(8,128)(2,1)S(1)}, u32[]{:S(2)}, u32[]{:S(2)}) %collective-permute-start.7) | collective-permute-done | bytes 917536 | tf_op jit(solution)/shard_map/ppermute | solution.py:17
  192.2 5.1 %collective-permute-done.2 = bf16[64,1792]{1,0:T(8,128)(2,1)S(1)} collective-permute-done((bf16[64,1792]{1,0:T(8,128)(2,1)S(1)}, bf16[64,1792]{1,0:T(8,128)(2,1)S(1)}, u32[]{:S(2)}, u32[]{:S(2)}) %collective-permute-start.2) | collective-permute-done | bytes 229408 | tf_op jit(solution)/shard_map/ppermute | solution.py:17
  198.5 3.2 collective-permute-start.20
  210.2 3.8 collective-permute-start.13
  214.7 5.3 %collective-permute-done.20 = bf16[256,1792]{1,0:T(8,128)(2,1)S(1)} collective-permute-done((bf16[256,1792]{1,0:T(8,128)(2,1)S(1)}, bf16[256,1792]{1,0:T(8,128)(2,1)S(1)}, u32[]{:S(2)}, u32[]{:S(2)}) %collective-permute-start.20) | collective-permute-done | bytes 917536 | tf_op jit(solution)/shard_map/ppermute | solution.py:17
  221.4 3.8 collective-permute-start.29
  227.8 4.5 %collective-permute-done.24 = bf16[512,256]{0,1:T(8,128)(2,1)S(1)} collective-permute-done((bf16[512,256]{0,1:T(8,128)(2,1)S(1)}, bf16[512,256]{0,1:T(8,128)(2,1)S(1)}, u32[]{:S(2)}, u32[]{:S(2)}) %collective-permute-start.24) | collective-permute-done | bytes 262176 | tf_op jit(solution)/shard_map/ppermute | solution.py:17
  236.2 5.4 %collective-permute-done.29 = bf16[256,1792]{1,0:T(8,128)(2,1)S(1)} collective-permute-done((bf16[256,1792]{1,0:T(8,128)(2,1)S(1)}, bf16[256,1792]{1,0:T(8,128)(2,1)S(1)}, u32[]{:S(2)}, u32[]{:S(2)}) %collective-permute-start.29) | collective-permute-done | bytes 917536 | tf_op jit(solution)/shard_map/ppermute | solution.py:17
  246.5 3.6 collective-permute-start.38
  251.3 3.6 collective-permute-start.34
  254.9 16.8 %collective-permute-done.31 = bf16[512,256]{0,1:T(8,128)(2,1)S(1)} collective-permute-done((bf16[512,256]{0,1:T(8,128)(2,1)S(1)}, bf16[512,256]{0,1:T(8,128)(2,1)S(1)}, u32[]{:S(2)}, u32[]{:S(2)}) %collective-permute-start.31) | collective-permute-done | bytes 262176 | tf_op jit(solution)/shard_map/ppermute | solution.py:17
  275.1 4.6 %collective-permute-start.27 = (bf16[512,256]{0,1:T(8,128)(2,1)S(1)}, bf16[512,256]{0,1:T(8,128)(2,1)S(1)}, u32[]{:S(2)}, u32[]{:S(2)}) collective-permute-start(bf16[512,256]{0,1:T(8,128)(2,1)S(1)} %fusion.52), channel_id=1, source_target_pairs={{0,16},{1,17},{2,18},{3,19},{4,20},{5,21},{6,22},{7,23},{8,24},{9,... | collective-permute-start | bytes 786440 | tf_op jit(solution)/shard_map/ppermute | solution.py:17
  279.8 6.8 %collective-permute-done.32 = bf16[512,512]{0,1:T(8,128)(2,1)S(1)} collective-permute-done((bf16[512,512]{0,1:T(8,128)(2,1)S(1)}, bf16[512,512]{0,1:T(8,128)(2,1)S(1)}, u32[]{:S(2)}, u32[]{:S(2)}) %collective-permute-start.32) | collective-permute-done | bytes 524320 | tf_op jit(solution)/shard_map/ppermute | solution.py:17
  290.3 3.2 collective-permute-start.36
  302.4 3.5 collective-permute-start.47
  307.5 5.9 %collective-permute-done.47 = bf16[256,896]{1,0:T(8,128)(2,1)S(1)} collective-permute-done((bf16[256,896]{1,0:T(8,128)(2,1)S(1)}, bf16[256,896]{1,0:T(8,128)(2,1)S(1)}, u32[]{:S(2)}, u32[]{:S(2)}) %collective-permute-start.47) | collective-permute-done | bytes 458784 | tf_op jit(solution)/shard_map/ppermute | solution.py:17
  317.5 9.2 %collective-permute-done.51 = bf16[256,256]{1,0:T(8,128)(2,1)S(1)} collective-permute-done((bf16[256,256]{1,0:T(8,128)(2,1)S(1)}, bf16[256,256]{1,0:T(8,128)(2,1)S(1)}, u32[]{:S(2)}, u32[]{:S(2)}) %collective-permute-start.51) | collective-permute-done | bytes 131104 | tf_op jit(solution)/shard_map/ppermute | solution.py:17
  327.3 8.7 %collective-permute-done.49 = bf16[256,256]{1,0:T(8,128)(2,1)S(1)} collective-permute-done((bf16[256,256]{1,0:T(8,128)(2,1)S(1)}, bf16[256,256]{1,0:T(8,128)(2,1)S(1)}, u32[]{:S(2)}, u32[]{:S(2)}) %collective-permute-start.49) | collective-permute-done | bytes 131104 | tf_op jit(solution)/shard_map/ppermute | solution.py:17
  348.9 3.8 collective-permute-done.55
  357.9 5.6 %collective-permute-done.46 = bf16[512,256]{0,1:T(8,128)(2,1)S(1)} collective-permute-done((bf16[512,256]{0,1:T(8,128)(2,1)S(1)}, bf16[512,256]{0,1:T(8,128)(2,1)S(1)}, u32[]{:S(2)}, u32[]{:S(2)}) %collective-permute-start.46) | collective-permute-done | bytes 262176 | tf_op jit(solution)/shard_map/ppermute | solution.py:17
  370.3 5.5 %collective-permute-done.66 = bf16[256,896]{1,0:T(8,128)(2,1)S(1)} collective-permute-done((bf16[256,896]{1,0:T(8,128)(2,1)S(1)}, bf16[256,896]{1,0:T(8,128)(2,1)S(1)}, u32[]{:S(2)}, u32[]{:S(2)}) %collective-permute-start.66) | collective-permute-done | bytes 458784 | tf_op jit(solution)/shard_map/ppermute | solution.py:17
  375.8 3.7 collective-permute-start.60
  381.1 7.3 %collective-permute-done.63 = bf16[256,896]{1,0:T(8,128)(2,1)S(1)} collective-permute-done((bf16[256,896]{1,0:T(8,128)(2,1)S(1)}, bf16[256,896]{1,0:T(8,128)(2,1)S(1)}, u32[]{:S(2)}, u32[]{:S(2)}) %collective-permute-start.63) | collective-permute-done | bytes 458784 | tf_op jit(solution)/shard_map/ppermute | solution.py:17
  391.2 7.7 %collective-permute-done.67 = bf16[256,896]{1,0:T(8,128)(2,1)S(1)} collective-permute-done((bf16[256,896]{1,0:T(8,128)(2,1)S(1)}, bf16[256,896]{1,0:T(8,128)(2,1)S(1)}, u32[]{:S(2)}, u32[]{:S(2)}) %collective-permute-start.67) | collective-permute-done | bytes 458784 | tf_op jit(solution)/shard_map/ppermute | solution.py:17
  398.9 3.8 collective-permute-start.61
  407.1 6.5 %collective-permute-done.68 = bf16[256,896]{1,0:T(8,128)(2,1)S(1)} collective-permute-done((bf16[256,896]{1,0:T(8,128)(2,1)S(1)}, bf16[256,896]{1,0:T(8,128)(2,1)S(1)}, u32[]{:S(2)}, u32[]{:S(2)}) %collective-permute-start.68) | collective-permute-done | bytes 458784 | tf_op jit(solution)/shard_map/ppermute | solution.py:17
  430.0 3.3 collective-permute-done.59
  440.2 4.9 %collective-permute-done.72 = bf16[64,1792]{1,0:T(8,128)(2,1)S(1)} collective-permute-done((bf16[64,1792]{1,0:T(8,128)(2,1)S(1)}, bf16[64,1792]{1,0:T(8,128)(2,1)S(1)}, u32[]{:S(2)}, u32[]{:S(2)}) %collective-permute-start.72) | collective-permute-done | bytes 229408 | tf_op jit(solution)/shard_map/ppermute | solution.py:17
  (240 shorter events, 135.3 us)
Async XLA Ops:
  0.0 110.4 %collective-permute-start = (bf16[64,7168]{1,0:T(8,128)(2,1)}, bf16[64,7168]{1,0:T(8,128)(2,1)S(1)}, u32[]{:S(2)}, u32[]{:S(2)}) collective-permute-start(bf16[64,7168]{1,0:T(8,128)(2,1)} %bitcast.108), channel_id=1, source_target_pairs={{0,32},{32,64},{64,96},{96,128},{128,160},{160,192},{192,224},{224... | collective-permute-start | bytes 2752520 | tf_op jit(solution)/shard_map/ppermute | solution.py:22
  4.1 109.3 %collective-permute-start.4 = (bf16[1792,256]{1,0:T(8,128)(2,1)}, bf16[1792,256]{1,0:T(8,128)(2,1)}, u32[]{:S(2)}, u32[]{:S(2)}) collective-permute-start(bf16[1792,256]{1,0:T(8,128)(2,1)} %get-tuple-element.17), channel_id=1, source_target_pairs={{0,24},{1,25},{2,26},{3,27},{4,28},{5,29},{6,30},{7,31},{8,0},{9,1... | collective-permute-start | bytes 2752520 | tf_op jit(solution)/shard_map/ppermute | solution.py:17
  7.1 108.9 %collective-permute-start.10 = (bf16[1792,256]{1,0:T(8,128)(2,1)}, bf16[1792,256]{1,0:T(8,128)(2,1)}, u32[]{:S(2)}, u32[]{:S(2)}) collective-permute-start(bf16[1792,256]{1,0:T(8,128)(2,1)} %get-tuple-element.18), channel_id=1, source_target_pairs={{0,8},{1,9},{2,10},{3,11},{4,12},{5,13},{6,14},{7,15},{8,16},{9,17... | collective-permute-start | bytes 2752520 | tf_op jit(solution)/shard_map/ppermute | solution.py:17
  7.1 111.0 %collective-permute-start.6 = (bf16[1792,256]{1,0:T(8,128)(2,1)}, bf16[1792,256]{1,0:T(8,128)(2,1)S(1)}, u32[]{:S(2)}, u32[]{:S(2)}) collective-permute-start(bf16[1792,256]{1,0:T(8,128)(2,1)} %get-tuple-element.19), channel_id=1, source_target_pairs={{0,16},{1,17},{2,18},{3,19},{4,20},{5,21},{6,22},{7,23},{8,24},{9,... | collective-permute-start | bytes 2752520 | tf_op jit(solution)/shard_map/ppermute | solution.py:17
  11.3 109.7 %collective-permute-start.5 = (bf16[1792,256]{1,0:T(8,128)(2,1)}, bf16[1792,256]{1,0:T(8,128)(2,1)S(1)}, u32[]{:S(2)}, u32[]{:S(2)}) collective-permute-start(bf16[1792,256]{1,0:T(8,128)(2,1)} %get-tuple-element.21), channel_id=1, source_target_pairs={{0,24},{1,25},{2,26},{3,27},{4,28},{5,29},{6,30},{7,31},{8,0},{9,1... | collective-permute-start | bytes 2752520 | tf_op jit(solution)/shard_map/ppermute | solution.py:17
  110.4 24.9 %collective-permute-start.11 = (bf16[1792,256]{1,0:T(8,128)(2,1)S(1)}, bf16[1792,256]{1,0:T(8,128)(2,1)S(1)}, u32[]{:S(2)}, u32[]{:S(2)}) collective-permute-start(bf16[1792,256]{1,0:T(8,128)(2,1)S(1)} %copy-done.6), channel_id=1, source_target_pairs={{0,8},{1,9},{2,10},{3,11},{4,12},{5,13},{6,14},{7,15},{8,16},{9,17... | collective-permute-start | bytes 2752520 | tf_op jit(solution)/shard_map/ppermute | solution.py:17
  113.4 23.4 %collective-permute-start.17 = (bf16[256,1792]{1,0:T(8,128)(2,1)S(1)}, bf16[256,1792]{1,0:T(8,128)(2,1)S(1)}, u32[]{:S(2)}, u32[]{:S(2)}) collective-permute-start(bf16[256,1792]{1,0:T(8,128)(2,1)S(1)} %get-tuple-element.25), channel_id=1, source_target_pairs={{0,24},{1,25},{2,26},{3,27},{4,28},{5,29},{6,30},{7,31},{8,0},{9,1... | collective-permute-start | bytes 2752520 | tf_op jit(solution)/shard_map/ppermute | solution.py:17
  116.0 62.8 %collective-permute-start.19 = (bf16[256,1792]{1,0:T(8,128)(2,1)S(1)}, bf16[256,1792]{1,0:T(8,128)(2,1)S(1)}, u32[]{:S(2)}, u32[]{:S(2)}) collective-permute-start(bf16[256,1792]{1,0:T(8,128)(2,1)S(1)} %get-tuple-element.26), channel_id=1, source_target_pairs={{0,8},{1,9},{2,10},{3,11},{4,12},{5,13},{6,14},{7,15},{8,16},{9,17... | collective-permute-start | bytes 2752520 | tf_op jit(solution)/shard_map/ppermute | solution.py:17
  118.1 60.8 %collective-permute-start.18 = (bf16[256,1792]{1,0:T(8,128)(2,1)S(1)}, bf16[256,1792]{1,0:T(8,128)(2,1)S(1)}, u32[]{:S(2)}, u32[]{:S(2)}) collective-permute-start(bf16[256,1792]{1,0:T(8,128)(2,1)S(1)} %get-tuple-element.27), channel_id=1, source_target_pairs={{0,16},{1,17},{2,18},{3,19},{4,20},{5,21},{6,22},{7,23},{8,24},{9,... | collective-permute-start | bytes 2752520 | tf_op jit(solution)/shard_map/ppermute | solution.py:17
  121.0 70.0 %collective-permute-start.7 = (bf16[1792,256]{1,0:T(8,128)(2,1)S(1)}, bf16[1792,256]{1,0:T(8,128)(2,1)S(1)}, u32[]{:S(2)}, u32[]{:S(2)}) collective-permute-start(bf16[1792,256]{1,0:T(8,128)(2,1)S(1)} %copy-done.5), channel_id=1, source_target_pairs={{0,16},{1,17},{2,18},{3,19},{4,20},{5,21},{6,22},{7,23},{8,24},{9,... | collective-permute-start | bytes 2752520 | tf_op jit(solution)/shard_map/ppermute | solution.py:17
  135.3 56.9 %collective-permute-start.3 = (bf16[64,1792]{1,0:T(8,128)(2,1)S(1)}, bf16[64,1792]{1,0:T(8,128)(2,1)S(1)}, u32[]{:S(2)}, u32[]{:S(2)}) collective-permute-start(bf16[64,1792]{1,0:T(8,128)(2,1)S(1)} %get-tuple-element.32), channel_id=1, source_target_pairs={{0,8},{1,9},{2,10},{3,11},{4,12},{5,13},{6,14},{7,15},{8,16},{9,17... | collective-permute-start | bytes 688136 | tf_op jit(solution)/shard_map/ppermute | solution.py:17
  136.8 60.5 %collective-permute-start.2 = (bf16[64,1792]{1,0:T(8,128)(2,1)S(1)}, bf16[64,1792]{1,0:T(8,128)(2,1)S(1)}, u32[]{:S(2)}, u32[]{:S(2)}) collective-permute-start(bf16[64,1792]{1,0:T(8,128)(2,1)S(1)} %get-tuple-element.33), channel_id=1, source_target_pairs={{0,16},{1,17},{2,18},{3,19},{4,20},{5,21},{6,22},{7,23},{8,24},{9,... | collective-permute-start | bytes 688136 | tf_op jit(solution)/shard_map/ppermute | solution.py:17
  178.8 18.6 %collective-permute-start.1 = (bf16[64,1792]{1,0:T(8,128)(2,1)S(1)}, bf16[64,1792]{1,0:T(8,128)(2,1)S(1)}, u32[]{:S(2)}, u32[]{:S(2)}) collective-permute-start(bf16[64,1792]{1,0:T(8,128)(2,1)S(1)} %get-tuple-element.34), channel_id=1, source_target_pairs={{0,24},{1,25},{2,26},{3,27},{4,28},{5,29},{6,30},{7,31},{8,0},{9,1... | collective-permute-start | bytes 688136 | tf_op jit(solution)/shard_map/ppermute | solution.py:17
  198.4 21.7 %collective-permute-start.21 = (bf16[256,1792]{1,0:T(8,128)(2,1)S(1)}, bf16[256,1792]{1,0:T(8,128)(2,1)S(1)}, u32[]{:S(2)}, u32[]{:S(2)}) collective-permute-start(bf16[256,1792]{1,0:T(8,128)(2,1)S(1)} %bitcast.92), channel_id=1, source_target_pairs={{0,1},{1,2},{2,3},{3,4},{4,5},{5,6},{6,7},{7,0},{8,9},{9,10},{10,1... | collective-permute-start | bytes 2752520 | tf_op jit(solution)/shard_map/ppermute | solution.py:17
  198.5 21.5 %collective-permute-start.20 = (bf16[256,1792]{1,0:T(8,128)(2,1)S(1)}, bf16[256,1792]{1,0:T(8,128)(2,1)S(1)}, u32[]{:S(2)}, u32[]{:S(2)}) collective-permute-start(bf16[256,1792]{1,0:T(8,128)(2,1)S(1)} %bitcast.93), channel_id=1, source_target_pairs={{0,7},{1,0},{2,1},{3,2},{4,3},{5,4},{6,5},{7,6},{8,15},{9,8},{10,9... | collective-permute-start | bytes 2752520 | tf_op jit(solution)/shard_map/ppermute | solution.py:17
  221.4 20.3 %collective-permute-start.29 = (bf16[256,1792]{1,0:T(8,128)(2,1)S(1)}, bf16[256,1792]{1,0:T(8,128)(2,1)S(1)}, u32[]{:S(2)}, u32[]{:S(2)}) collective-permute-start(bf16[256,1792]{1,0:T(8,128)(2,1)S(1)} %collective-permute-done.20), channel_id=1, source_target_pairs={{0,7},{1,0},{2,1},{3,2},{4,3},{5,4},{6,5},{7,6},{8,15},{9,8},{10,9... | collective-permute-start | bytes 2752520 | tf_op jit(solution)/shard_map/ppermute | solution.py:17
  225.3 16.5 %collective-permute-start.30 = (bf16[256,1792]{1,0:T(8,128)(2,1)S(1)}, bf16[256,1792]{1,0:T(8,128)(2,1)S(1)}, u32[]{:S(2)}, u32[]{:S(2)}) collective-permute-start(bf16[256,1792]{1,0:T(8,128)(2,1)S(1)} %collective-permute-done.21), channel_id=1, source_target_pairs={{0,1},{1,2},{2,3},{3,4},{4,5},{5,6},{6,7},{7,0},{8,9},{9,10},{10,1... | collective-permute-start | bytes 2752520 | tf_op jit(solution)/shard_map/ppermute | solution.py:17
  225.6 17.5 %collective-permute-start.22 = (bf16[512,256]{0,1:T(8,128)(2,1)S(1)}, bf16[512,256]{0,1:T(8,128)(2,1)S(1)}, u32[]{:S(2)}, u32[]{:S(2)}) collective-permute-start(bf16[512,256]{0,1:T(8,128)(2,1)S(1)} %get-tuple-element.36), channel_id=1, source_target_pairs={{0,8},{1,9},{2,10},{3,11},{4,12},{5,13},{6,14},{7,15},{8,16},{9,17... | collective-permute-start | bytes 786440 | tf_op jit(solution)/shard_map/ppermute | solution.py:17
  233.5 39.4 %collective-permute-start.25 = (bf16[512,512]{0,1:T(8,128)(2,1)S(1)}, bf16[512,512]{0,1:T(8,128)(2,1)S(1)}, u32[]{:S(2)}, u32[]{:S(2)}) collective-permute-start(bf16[512,512]{0,1:T(8,128)(2,1)S(1)} %fusion.10), channel_id=1, source_target_pairs={{0,24},{1,25},{2,26},{3,27},{4,28},{5,29},{6,30},{7,31},{8,0},{9,1... | collective-permute-start | bytes 1572872 | tf_op jit(solution)/shard_map/ppermute | solution.py:17
  244.3 28.7 %collective-permute-start.23 = (bf16[512,512]{0,1:T(8,128)(2,1)S(1)}, bf16[512,512]{0,1:T(8,128)(2,1)S(1)}, u32[]{:S(2)}, u32[]{:S(2)}) collective-permute-start(bf16[512,512]{0,1:T(8,128)(2,1)S(1)} %fusion.9), channel_id=1, source_target_pairs={{0,8},{1,9},{2,10},{3,11},{4,12},{5,13},{6,14},{7,15},{8,16},{9,17... | collective-permute-start | bytes 1572872 | tf_op jit(solution)/shard_map/ppermute | solution.py:17
  246.4 25.3 %collective-permute-start.31 = (bf16[512,256]{0,1:T(8,128)(2,1)S(1)}, bf16[512,256]{0,1:T(8,128)(2,1)S(1)}, u32[]{:S(2)}, u32[]{:S(2)}) collective-permute-start(bf16[512,256]{0,1:T(8,128)(2,1)S(1)} %get-tuple-element.38), channel_id=1, source_target_pairs={{0,8},{1,9},{2,10},{3,11},{4,12},{5,13},{6,14},{7,15},{8,16},{9,17... | collective-permute-start | bytes 786440 | tf_op jit(solution)/shard_map/ppermute | solution.py:17
  246.5 41.4 %collective-permute-start.38 = (bf16[256,1792]{1,0:T(8,128)(2,1)S(1)}, bf16[256,1792]{1,0:T(8,128)(2,1)S(1)}, u32[]{:S(2)}, u32[]{:S(2)}) collective-permute-start(bf16[256,1792]{1,0:T(8,128)(2,1)S(1)} %collective-permute-done.29), channel_id=1, source_target_pairs={{0,7},{1,0},{2,1},{3,2},{4,3},{5,4},{6,5},{7,6},{8,15},{9,8},{10,9... | collective-permute-start | bytes 2752520 | tf_op jit(solution)/shard_map/ppermute | solution.py:17
  251.3 23.8 %collective-permute-start.34 = (bf16[512,512]{0,1:T(8,128)(2,1)S(1)}, bf16[512,512]{0,1:T(8,128)(2,1)S(1)}, u32[]{:S(2)}, u32[]{:S(2)}) collective-permute-start(bf16[512,512]{0,1:T(8,128)(2,1)S(1)} %fusion.12), channel_id=1, source_target_pairs={{0,24},{1,25},{2,26},{3,27},{4,28},{5,29},{6,30},{7,31},{8,0},{9,1... | collective-permute-start | bytes 1572872 | tf_op jit(solution)/shard_map/ppermute | solution.py:17
  275.0 19.8 %collective-permute-start.28 = (bf16[512,256]{0,1:T(8,128)(2,1)S(1)}, bf16[512,256]{0,1:T(8,128)(2,1)S(1)}, u32[]{:S(2)}, u32[]{:S(2)}) collective-permute-start(bf16[512,256]{0,1:T(8,128)(2,1)S(1)} %fusion.52), channel_id=1, source_target_pairs={{0,8},{1,9},{2,10},{3,11},{4,12},{5,13},{6,14},{7,15},{8,16},{9,17... | collective-permute-start | bytes 786440 | tf_op jit(solution)/shard_map/ppermute | solution.py:17
  275.1 19.8 %collective-permute-start.27 = (bf16[512,256]{0,1:T(8,128)(2,1)S(1)}, bf16[512,256]{0,1:T(8,128)(2,1)S(1)}, u32[]{:S(2)}, u32[]{:S(2)}) collective-permute-start(bf16[512,256]{0,1:T(8,128)(2,1)S(1)} %fusion.52), channel_id=1, source_target_pairs={{0,16},{1,17},{2,18},{3,19},{4,20},{5,21},{6,22},{7,23},{8,24},{9,... | collective-permute-start | bytes 786440 | tf_op jit(solution)/shard_map/ppermute | solution.py:17
  295.0 125.6 %collective-permute-start.16 = (bf16[256,256]{1,0:T(8,128)(2,1)S(1)}, bf16[256,256]{1,0:T(8,128)(2,1)S(1)}, u32[]{:S(2)}, u32[]{:S(2)}) collective-permute-start(bf16[256,256]{1,0:T(8,128)(2,1)S(1)} %fusion.84), channel_id=1, source_target_pairs={{0,8},{1,9},{2,10},{3,11},{4,12},{5,13},{6,14},{7,15},{8,16},{9,17... | collective-permute-start | bytes 393224 | tf_op jit(solution)/shard_map/ppermute | solution.py:17
  301.5 121.1 %collective-permute-start.15 = (bf16[256,256]{1,0:T(8,128)(2,1)S(1)}, bf16[256,256]{1,0:T(8,128)(2,1)S(1)}, u32[]{:S(2)}, u32[]{:S(2)}) collective-permute-start(bf16[256,256]{1,0:T(8,128)(2,1)S(1)} %fusion.84), channel_id=1, source_target_pairs={{0,16},{1,17},{2,18},{3,19},{4,20},{5,21},{6,22},{7,23},{8,24},{9,... | collective-permute-start | bytes 393224 | tf_op jit(solution)/shard_map/ppermute | solution.py:17
  313.4 23.3 %collective-permute-start.43 = (bf16[512,512]{0,1:T(8,128)(2,1)S(1)}, bf16[512,512]{0,1:T(8,128)(2,1)S(1)}, u32[]{:S(2)}, u32[]{:S(2)}) collective-permute-start(bf16[512,512]{0,1:T(8,128)(2,1)S(1)} %fusion.14), channel_id=1, source_target_pairs={{0,24},{1,25},{2,26},{3,27},{4,28},{5,29},{6,30},{7,31},{8,0},{9,1... | collective-permute-start | bytes 1572872 | tf_op jit(solution)/shard_map/ppermute | solution.py:17
  317.4 21.4 %collective-permute-start.41 = (bf16[512,512]{0,1:T(8,128)(2,1)S(1)}, bf16[512,512]{0,1:T(8,128)(2,1)S(1)}, u32[]{:S(2)}, u32[]{:S(2)}) collective-permute-start(bf16[512,512]{0,1:T(8,128)(2,1)S(1)} %fusion.13), channel_id=1, source_target_pairs={{0,8},{1,9},{2,10},{3,11},{4,12},{5,13},{6,14},{7,15},{8,16},{9,17... | collective-permute-start | bytes 1572872 | tf_op jit(solution)/shard_map/ppermute | solution.py:17
  366.9 21.4 %collective-permute-start.63 = (bf16[256,896]{1,0:T(8,128)(2,1)S(1)}, bf16[256,896]{1,0:T(8,128)(2,1)S(1)}, u32[]{:S(2)}, u32[]{:S(2)}) collective-permute-start(bf16[256,896]{1,0:T(8,128)(2,1)S(1)} %convolution_convert_fusion.4), channel_id=1, source_target_pairs={{0,1},{1,2},{2,3},{3,4},{4,5},{5,6},{6,7},{7,0},{8,9},{9,10},{10,1... | collective-permute-start | bytes 1376264 | tf_op jit(solution)/shard_map/ppermute | solution.py:17
  380.2 18.7 %collective-permute-start.67 = (bf16[256,896]{1,0:T(8,128)(2,1)S(1)}, bf16[256,896]{1,0:T(8,128)(2,1)S(1)}, u32[]{:S(2)}, u32[]{:S(2)}) collective-permute-start(bf16[256,896]{1,0:T(8,128)(2,1)S(1)} %fusion.24), channel_id=1, source_target_pairs={{0,7},{1,0},{2,1},{3,2},{4,3},{5,4},{6,5},{7,6},{8,15},{9,8},{10,9... | collective-permute-start | bytes 1376264 | tf_op jit(solution)/shard_map/ppermute | solution.py:17
  398.9 17.4 %collective-permute-start.61 = (bf16[256,896]{1,0:T(8,128)(2,1)S(1)}, bf16[256,896]{1,0:T(8,128)(2,1)S(1)}, u32[]{:S(2)}, u32[]{:S(2)}) collective-permute-start(bf16[256,896]{1,0:T(8,128)(2,1)S(1)} %fusion.19), channel_id=1, source_target_pairs={{0,7},{1,0},{2,1},{3,2},{4,3},{5,4},{6,5},{7,6},{8,15},{9,8},{10,9... | collective-permute-start | bytes 1376264 | tf_op jit(solution)/shard_map/ppermute | solution.py:17
  (53 other events, 739.1 us)
